TPU v7x, 512 devices: a whole 4x8x8 slice. The times are simulated.
512 devices in a mesh: gene: 32 (over z_hi, y), cell: 16 (over z_lo, x, core).
Axes of the slice: x: 4, y: 8, z: 8 (z_hi: 4, z_lo: 2; z = z_hi * 2 + z_lo), core: 2. Of those that a mesh axis runs over, the one named last changes fastest.
Arguments:
- expression: float32 [4096, 12288], P('cell', 'gene'), may hold values from -40 to 48
Outputs:
- band: float32 [12288, 2688], P(('gene', 'cell'))
All inputs are finite; a program needn't handle non-finite values.
Results may differ from a plain program's by a relative error of at most 0.00065.
Values may be sent and summed in bfloat16 or wider, within the bound.
A program may use at most 64 MiB of HBM per device.

v0:
```python
import jax
import jax.numpy as jnp
from jax import lax
from jax.sharding import PartitionSpec as P

SLICES = 4
REACH = 3


EPS = 1e-05
RADIX = 4.0


def from_behind(value, axis, steps):
    count = lax.axis_size(axis)
    pairs = [(source, (source + steps) % count) for source in range(count)]
    return lax.ppermute(value, axis, pairs)


def slice_panels(standard, scale):
    rest = standard * scale
    pieces = []
    for level in range(SLICES):
        grown = rest * RADIX
        piece = jnp.floor(grown)
        pieces.append(piece)
        rest = grown - piece
    return jnp.stack(pieces).astype(jnp.bfloat16)


def contract_cells(left, right):
    return lax.dot_general(
        left, right, (((0,), (0,)), ((), ())), preferred_element_type=jnp.float32
    )


def truncated_value(panels):
    total = jnp.zeros(panels.shape[1:], jnp.float32)
    for level in range(SLICES):
        total = total + panels[level].astype(jnp.float32) * RADIX ** (-(level + 1))
    return total.astype(jnp.bfloat16)


def block_product(own_panels, own_scale, item, cells_total):
    far_value, far_power = item
    far_scale = jnp.exp2(-far_power.astype(jnp.float32))
    far_panels = slice_panels(far_value.astype(jnp.float32), 1.0)
    product = jnp.zeros((own_panels.shape[2], far_panels.shape[2]), jnp.float32)
    for first in range(SLICES):
        for second in range(SLICES - first):
            term = contract_cells(own_panels[first], far_panels[second])
            product = product + term * RADIX ** (-(first + second + 2))
    return product / (own_scale[:, None] * far_scale[None, :] * cells_total)


def on_device(expression):
    cells_total = float(expression.shape[0] * lax.axis_size("cell"))
    total = lax.psum(jnp.sum(expression, axis=0), "cell")
    mean = total / cells_total
    centred = expression - mean
    spread = lax.psum(jnp.sum(centred * centred, axis=0), "cell")
    standard = centred / jnp.sqrt(spread / cells_total + EPS)
    peak = lax.pmax(jnp.max(jnp.abs(standard), axis=0), "cell")
    power = jnp.ceil(jnp.log2(peak))
    own_scale = jnp.exp2(-power)
    own_panels = slice_panels(standard, own_scale)
    carried = (truncated_value(own_panels), power.astype(jnp.bfloat16))
    blocks = {}
    current = from_behind((carried[0], carried[1]), "gene", REACH)
    blocks[0] = block_product(own_panels, own_scale, current, cells_total)
    for step in range(1, 2 * REACH + 1):
        current = from_behind((current[0], current[1]), "gene", -1)
        blocks[step] = block_product(own_panels, own_scale, current, cells_total)
    whole = jnp.concatenate([blocks[slot] for slot in range(2 * REACH + 1)], axis=1)
    return lax.psum_scatter(whole, "cell", scatter_dimension=0, tiled=True)


def solution(mesh):
    placed = (P("cell", "gene"),)
    return jax.shard_map(
        on_device, mesh=mesh, in_specs=placed, out_specs=P(("gene", "cell"), None), check_vma=False
    )
```

profile of v0, /device:TPU:1, one launch (start us, length us, event | category | flops | bytes accessed | tf_op | source)
XLA Modules:
  0.0 400.5 jit_solution(627287739506168523)
XLA Ops:
  7.6 33.4 %psum.14 = f32[384]{0:T(512)S(1)} all-reduce(f32[384]{0:T(512)S(1)} %reduce_sum.18), channel_id=1, replica_groups=mesh['gene'=32,'cell'=16] {'cell'}, use_global_device_ids=true, to_apply=%region_1.0 | all-reduce | flops 384 | bytes 3072 | tf_op jit(solution)/shard_map/psum | solution.py:58
  41.0 1.1 multiply_reduce_fusion
  42.0 27.1 %psum.15 = f32[384]{0:T(512)S(1)} all-reduce(f32[384]{0:T(512)S(1)} %multiply_reduce_fusion), channel_id=1, replica_groups=mesh['gene'=32,'cell'=16] {'cell'}, use_global_device_ids=true, to_apply=%region_3.0 | all-reduce | flops 384 | bytes 3072 | tf_op jit(solution)/shard_map/psum | solution.py:61
  69.2 1.1 abs_reduce_fusion
  70.2 27.1 %pmax.7 = f32[384]{0:T(512)S(1)} all-reduce(f32[384]{0:T(512)S(1)} %abs_reduce_fusion), channel_id=1, replica_groups=mesh['gene'=32,'cell'=16] {'cell'}, use_global_device_ids=true, to_apply=%region_5.0 | all-reduce | flops 384 | bytes 3072 | tf_op jit(solution)/shard_map/pmax | solution.py:63
  97.4 3.9 collective-permute-start.1
  101.2 1.3 add_convert_fusion
  102.6 4.6 %collective-permute-start = (bf16[256,384]{1,0:T(8,128)(2,1)S(1)}, bf16[256,384]{1,0:T(8,128)(2,1)S(1)}, u32[]{:S(2)}, u32[]{:S(2)}) collective-permute-start(bf16[256,384]{1,0:T(8,128)(2,1)S(1)} %get-tuple-element.5), channel_id=1, source_target_pairs={{0,48},{16,64},{32,80},{48,96},{64,112},{80,128},{96,144},{112,160... | collective-permute-start | bytes 589832 | tf_op jit(solution)/shard_map/ppermute | solution.py:17
  107.2 4.0 collective-permute-done.1
  111.2 3.6 collective-permute-start.3
  115.8 7.5 %collective-permute-start.5 = (bf16[384]{0:T(512)(128)(2,1)S(1)}, bf16[384]{0:T(512)(128)(2,1)S(1)}, u32[]{:S(2)}, u32[]{:S(2)}) collective-permute-start(bf16[384]{0:T(512)(128)(2,1)S(1)} %collective-permute-done.3), channel_id=1, source_target_pairs={{0,496},{16,0},{32,16},{48,32},{64,48},{80,64},{96,80},{112,96},{1... | collective-permute-start | bytes 2312 | tf_op jit(solution)/shard_map/ppermute | solution.py:17
  124.0 7.8 %collective-permute-start.7 = (bf16[384]{0:T(512)(128)(2,1)S(1)}, bf16[384]{0:T(512)(128)(2,1)S(1)}, u32[]{:S(2)}, u32[]{:S(2)}) collective-permute-start(bf16[384]{0:T(512)(128)(2,1)S(1)} %collective-permute-done.5), channel_id=1, source_target_pairs={{0,496},{16,0},{32,16},{48,32},{64,48},{80,64},{96,80},{112,96},{1... | collective-permute-start | bytes 2312 | tf_op jit(solution)/shard_map/ppermute | solution.py:17
  132.5 7.8 %collective-permute-start.9 = (bf16[384]{0:T(512)(128)(2,1)S(1)}, bf16[384]{0:T(512)(128)(2,1)S(1)}, u32[]{:S(2)}, u32[]{:S(2)}) collective-permute-start(bf16[384]{0:T(512)(128)(2,1)S(1)} %collective-permute-done.7), channel_id=1, source_target_pairs={{0,496},{16,0},{32,16},{48,32},{64,48},{80,64},{96,80},{112,96},{1... | collective-permute-start | bytes 2312 | tf_op jit(solution)/shard_map/ppermute | solution.py:17
  141.1 7.8 %collective-permute-start.11 = (bf16[384]{0:T(512)(128)(2,1)S(1)}, bf16[384]{0:T(512)(128)(2,1)S(1)}, u32[]{:S(2)}, u32[]{:S(2)}) collective-permute-start(bf16[384]{0:T(512)(128)(2,1)S(1)} %collective-permute-done.9), channel_id=1, source_target_pairs={{0,496},{16,0},{32,16},{48,32},{64,48},{80,64},{96,80},{112,96},{1... | collective-permute-start | bytes 2312 | tf_op jit(solution)/shard_map/ppermute | solution.py:17
  149.6 7.8 %collective-permute-start.13 = (bf16[384]{0:T(512)(128)(2,1)S(1)}, bf16[384]{0:T(512)(128)(2,1)S(1)}, u32[]{:S(2)}, u32[]{:S(2)}) collective-permute-start(bf16[384]{0:T(512)(128)(2,1)S(1)} %collective-permute-done.11), channel_id=1, source_target_pairs={{0,496},{16,0},{32,16},{48,32},{64,48},{80,64},{96,80},{112,96},{1... | collective-permute-start | bytes 2312 | tf_op jit(solution)/shard_map/ppermute | solution.py:17
  158.1 7.8 %collective-permute-start.2 = (bf16[256,384]{1,0:T(8,128)(2,1)S(1)}, bf16[256,384]{1,0:T(8,128)(2,1)S(1)}, u32[]{:S(2)}, u32[]{:S(2)}) collective-permute-start(bf16[256,384]{1,0:T(8,128)(2,1)S(1)} %collective-permute-done), channel_id=1, source_target_pairs={{0,496},{16,0},{32,16},{48,32},{64,48},{80,64},{96,80},{112,96},{1... | collective-permute-start | bytes 589832 | tf_op jit(solution)/shard_map/ppermute | solution.py:17
  169.0 1.1 fusion.68
  170.4 8.2 %collective-permute-start.4 = (bf16[256,384]{1,0:T(8,128)(2,1)S(1)}, bf16[256,384]{1,0:T(8,128)(2,1)S(1)}, u32[]{:S(2)}, u32[]{:S(2)}) collective-permute-start(bf16[256,384]{1,0:T(8,128)(2,1)S(1)} %collective-permute-done.2), channel_id=1, source_target_pairs={{0,496},{16,0},{32,16},{48,32},{64,48},{80,64},{96,80},{112,96},{1... | collective-permute-start | bytes 589832 | tf_op jit(solution)/shard_map/ppermute | solution.py:17
  181.4 1.2 fusion.57
  182.8 8.7 %collective-permute-start.6 = (bf16[256,384]{1,0:T(8,128)(2,1)S(1)}, bf16[256,384]{1,0:T(8,128)(2,1)S(1)}, u32[]{:S(2)}, u32[]{:S(2)}) collective-permute-start(bf16[256,384]{1,0:T(8,128)(2,1)S(1)} %collective-permute-done.4), channel_id=1, source_target_pairs={{0,496},{16,0},{32,16},{48,32},{64,48},{80,64},{96,80},{112,96},{1... | collective-permute-start | bytes 589832 | tf_op jit(solution)/shard_map/ppermute | solution.py:17
  194.2 1.2 fusion.46
  195.7 9.4 %collective-permute-start.8 = (bf16[256,384]{1,0:T(8,128)(2,1)S(1)}, bf16[256,384]{1,0:T(8,128)(2,1)S(1)}, u32[]{:S(2)}, u32[]{:S(2)}) collective-permute-start(bf16[256,384]{1,0:T(8,128)(2,1)S(1)} %collective-permute-done.6), channel_id=1, source_target_pairs={{0,496},{16,0},{32,16},{48,32},{64,48},{80,64},{96,80},{112,96},{1... | collective-permute-start | bytes 589832 | tf_op jit(solution)/shard_map/ppermute | solution.py:17
  207.8 1.1 fusion.35
  209.3 8.7 %collective-permute-start.10 = (bf16[256,384]{1,0:T(8,128)(2,1)S(1)}, bf16[256,384]{1,0:T(8,128)(2,1)S(1)}, u32[]{:S(2)}, u32[]{:S(2)}) collective-permute-start(bf16[256,384]{1,0:T(8,128)(2,1)S(1)} %collective-permute-done.8), channel_id=1, source_target_pairs={{0,496},{16,0},{32,16},{48,32},{64,48},{80,64},{96,80},{112,96},{1... | collective-permute-start | bytes 589832 | tf_op jit(solution)/shard_map/ppermute | solution.py:17
  220.7 1.2 fusion.24
  222.2 8.5 %collective-permute-start.12 = (bf16[256,384]{1,0:T(8,128)(2,1)S(1)}, bf16[256,384]{1,0:T(8,128)(2,1)S(1)}, u32[]{:S(2)}, u32[]{:S(2)}) collective-permute-start(bf16[256,384]{1,0:T(8,128)(2,1)S(1)} %collective-permute-done.10), channel_id=1, source_target_pairs={{0,496},{16,0},{32,16},{48,32},{64,48},{80,64},{96,80},{112,96},{1... | collective-permute-start | bytes 589832 | tf_op jit(solution)/shard_map/ppermute | solution.py:17
  233.4 1.1 fusion.13
  237.6 1.1 fusion.2
  238.7 1.3 dynamic-slice
  240.6 149.7 %all-reduce.3.cloned.1.call-done = f32[384,2688]{0,1:T(8,128)} async-done(((f32[384,2688]{0,1:T(8,128)}), f32[384,2688]{0,1:T(8,128)}) %all-reduce.3.cloned.1.call-update) | async-done | bytes 4128784
  390.3 2.2 constant_dynamic-slice_fusion
  392.5 1.1 copy.3
  (89 shorter events, 26.3 us)
Async XLA Ops:
  6.5 383.8 %all-reduce.3.cloned.1.call-start = ((), (), s32[]{:S(2)}) async-start(), calls=%async_computation | async-start | bytes 8257536
  97.4 13.8 %collective-permute-start.1 = (bf16[384]{0:T(512)(128)(2,1)S(1)}, bf16[384]{0:T(512)(128)(2,1)S(1)}, u32[]{:S(2)}, u32[]{:S(2)}) collective-permute-start(bf16[384]{0:T(512)(128)(2,1)S(1)} %get-tuple-element.10), channel_id=1, source_target_pairs={{0,48},{16,64},{32,80},{48,96},{64,112},{80,128},{96,144},{112,160... | collective-permute-start | bytes 2312 | tf_op jit(solution)/shard_map/ppermute | solution.py:17
  102.6 55.6 %collective-permute-start = (bf16[256,384]{1,0:T(8,128)(2,1)S(1)}, bf16[256,384]{1,0:T(8,128)(2,1)S(1)}, u32[]{:S(2)}, u32[]{:S(2)}) collective-permute-start(bf16[256,384]{1,0:T(8,128)(2,1)S(1)} %get-tuple-element.5), channel_id=1, source_target_pairs={{0,48},{16,64},{32,80},{48,96},{64,112},{80,128},{96,144},{112,160... | collective-permute-start | bytes 589832 | tf_op jit(solution)/shard_map/ppermute | solution.py:17
  111.2 4.6 %collective-permute-start.3 = (bf16[384]{0:T(512)(128)(2,1)S(1)}, bf16[384]{0:T(512)(128)(2,1)S(1)}, u32[]{:S(2)}, u32[]{:S(2)}) collective-permute-start(bf16[384]{0:T(512)(128)(2,1)S(1)} %collective-permute-done.1), channel_id=1, source_target_pairs={{0,496},{16,0},{32,16},{48,32},{64,48},{80,64},{96,80},{112,96},{1... | collective-permute-start | bytes 2312 | tf_op jit(solution)/shard_map/ppermute | solution.py:17
  115.8 8.2 %collective-permute-start.5 = (bf16[384]{0:T(512)(128)(2,1)S(1)}, bf16[384]{0:T(512)(128)(2,1)S(1)}, u32[]{:S(2)}, u32[]{:S(2)}) collective-permute-start(bf16[384]{0:T(512)(128)(2,1)S(1)} %collective-permute-done.3), channel_id=1, source_target_pairs={{0,496},{16,0},{32,16},{48,32},{64,48},{80,64},{96,80},{112,96},{1... | collective-permute-start | bytes 2312 | tf_op jit(solution)/shard_map/ppermute | solution.py:17
  124.0 8.5 %collective-permute-start.7 = (bf16[384]{0:T(512)(128)(2,1)S(1)}, bf16[384]{0:T(512)(128)(2,1)S(1)}, u32[]{:S(2)}, u32[]{:S(2)}) collective-permute-start(bf16[384]{0:T(512)(128)(2,1)S(1)} %collective-permute-done.5), channel_id=1, source_target_pairs={{0,496},{16,0},{32,16},{48,32},{64,48},{80,64},{96,80},{112,96},{1... | collective-permute-start | bytes 2312 | tf_op jit(solution)/shard_map/ppermute | solution.py:17
  132.5 8.5 %collective-permute-start.9 = (bf16[384]{0:T(512)(128)(2,1)S(1)}, bf16[384]{0:T(512)(128)(2,1)S(1)}, u32[]{:S(2)}, u32[]{:S(2)}) collective-permute-start(bf16[384]{0:T(512)(128)(2,1)S(1)} %collective-permute-done.7), channel_id=1, source_target_pairs={{0,496},{16,0},{32,16},{48,32},{64,48},{80,64},{96,80},{112,96},{1... | collective-permute-start | bytes 2312 | tf_op jit(solution)/shard_map/ppermute | solution.py:17
  141.1 8.5 %collective-permute-start.11 = (bf16[384]{0:T(512)(128)(2,1)S(1)}, bf16[384]{0:T(512)(128)(2,1)S(1)}, u32[]{:S(2)}, u32[]{:S(2)}) collective-permute-start(bf16[384]{0:T(512)(128)(2,1)S(1)} %collective-permute-done.9), channel_id=1, source_target_pairs={{0,496},{16,0},{32,16},{48,32},{64,48},{80,64},{96,80},{112,96},{1... | collective-permute-start | bytes 2312 | tf_op jit(solution)/shard_map/ppermute | solution.py:17
  149.6 8.5 %collective-permute-start.13 = (bf16[384]{0:T(512)(128)(2,1)S(1)}, bf16[384]{0:T(512)(128)(2,1)S(1)}, u32[]{:S(2)}, u32[]{:S(2)}) collective-permute-start(bf16[384]{0:T(512)(128)(2,1)S(1)} %collective-permute-done.11), channel_id=1, source_target_pairs={{0,496},{16,0},{32,16},{48,32},{64,48},{80,64},{96,80},{112,96},{1... | collective-permute-start | bytes 2312 | tf_op jit(solution)/shard_map/ppermute | solution.py:17
  158.1 12.0 %collective-permute-start.2 = (bf16[256,384]{1,0:T(8,128)(2,1)S(1)}, bf16[256,384]{1,0:T(8,128)(2,1)S(1)}, u32[]{:S(2)}, u32[]{:S(2)}) collective-permute-start(bf16[256,384]{1,0:T(8,128)(2,1)S(1)} %collective-permute-done), channel_id=1, source_target_pairs={{0,496},{16,0},{32,16},{48,32},{64,48},{80,64},{96,80},{112,96},{1... | collective-permute-start | bytes 589832 | tf_op jit(solution)/shard_map/ppermute | solution.py:17
  170.4 12.1 %collective-permute-start.4 = (bf16[256,384]{1,0:T(8,128)(2,1)S(1)}, bf16[256,384]{1,0:T(8,128)(2,1)S(1)}, u32[]{:S(2)}, u32[]{:S(2)}) collective-permute-start(bf16[256,384]{1,0:T(8,128)(2,1)S(1)} %collective-permute-done.2), channel_id=1, source_target_pairs={{0,496},{16,0},{32,16},{48,32},{64,48},{80,64},{96,80},{112,96},{1... | collective-permute-start | bytes 589832 | tf_op jit(solution)/shard_map/ppermute | solution.py:17
  182.8 12.5 %collective-permute-start.6 = (bf16[256,384]{1,0:T(8,128)(2,1)S(1)}, bf16[256,384]{1,0:T(8,128)(2,1)S(1)}, u32[]{:S(2)}, u32[]{:S(2)}) collective-permute-start(bf16[256,384]{1,0:T(8,128)(2,1)S(1)} %collective-permute-done.4), channel_id=1, source_target_pairs={{0,496},{16,0},{32,16},{48,32},{64,48},{80,64},{96,80},{112,96},{1... | collective-permute-start | bytes 589832 | tf_op jit(solution)/shard_map/ppermute | solution.py:17
  195.7 13.3 %collective-permute-start.8 = (bf16[256,384]{1,0:T(8,128)(2,1)S(1)}, bf16[256,384]{1,0:T(8,128)(2,1)S(1)}, u32[]{:S(2)}, u32[]{:S(2)}) collective-permute-start(bf16[256,384]{1,0:T(8,128)(2,1)S(1)} %collective-permute-done.6), channel_id=1, source_target_pairs={{0,496},{16,0},{32,16},{48,32},{64,48},{80,64},{96,80},{112,96},{1... | collective-permute-start | bytes 589832 | tf_op jit(solution)/shard_map/ppermute | solution.py:17
  209.3 12.6 %collective-permute-start.10 = (bf16[256,384]{1,0:T(8,128)(2,1)S(1)}, bf16[256,384]{1,0:T(8,128)(2,1)S(1)}, u32[]{:S(2)}, u32[]{:S(2)}) collective-permute-start(bf16[256,384]{1,0:T(8,128)(2,1)S(1)} %collective-permute-done.8), channel_id=1, source_target_pairs={{0,496},{16,0},{32,16},{48,32},{64,48},{80,64},{96,80},{112,96},{1... | collective-permute-start | bytes 589832 | tf_op jit(solution)/shard_map/ppermute | solution.py:17
  222.2 12.3 %collective-permute-start.12 = (bf16[256,384]{1,0:T(8,128)(2,1)S(1)}, bf16[256,384]{1,0:T(8,128)(2,1)S(1)}, u32[]{:S(2)}, u32[]{:S(2)}) collective-permute-start(bf16[256,384]{1,0:T(8,128)(2,1)S(1)} %collective-permute-done.10), channel_id=1, source_target_pairs={{0,496},{16,0},{32,16},{48,32},{64,48},{80,64},{96,80},{112,96},{1... | collective-permute-start | bytes 589832 | tf_op jit(solution)/shard_map/ppermute | solution.py:17
Sparse Core Ops, SparseCore 0:
  238.8 151.4 all-reduce.2
where the time goes:
time: 401 us; the launch traced here: 400 us
  waiting for transfers between devices  158 us (39%)
  starting transfers between devices  102 us (25%)
  blocking collectives  87.6 us (22%)
  matrix products  28.7 us (7%)
  between operations  14.7 us (4%)
  local copies, waits for them, and re-layouts  4.57 us (1%)
  other arithmetic  4.56 us (1%)
    unnamed x2, waiting for transfers between devices  150 us
    ppermute x14, starting transfers between devices, from_behind(): return lax.ppermute(value, axis, pairs)  102 us
    psum x1, blocking collectives, on_device(): total = lax.psum(jnp.sum(expression, axis=0), 'cell')  33.4 us
    dot_general x70, matrix products, contract_cells(): lax.dot_general(left, right, (((0,), (0,)), ((), ())), preferred_element_...  28.7 us
    pmax x1, blocking collectives, on_device(): peak = lax.pmax(jnp.max(jnp.abs(standard), axis=0), 'cell')  27.1 us
    psum x1, blocking collectives, on_device(): spread = lax.psum(jnp.sum(centred * centred, axis=0), 'cell')  27.1 us
    ppermute x14, waiting for transfers between devices, from_behind(): return lax.ppermute(value, axis, pairs)  8.44 us
  transfers between devices with their start and end apart: 15, of which 8 were waited for; matrix products, arithmetic and copies ran while one was open for 6% of the time, Pallas kernels for 0%

commit v1 on v0

v1 whole, which is shorter than its diff:
```python
import jax
import jax.numpy as jnp
from jax import lax
from jax.experimental import pallas as pl
from jax.experimental.pallas import tpu as pltpu
from jax.sharding import PartitionSpec as P

EPS = 1e-05
MESH = pl.DeviceIdType.MESH
N_GENE, N_CELL, N_CHIP = 32, 16, 8
GENES, CELLS, ROWS = 384, 256, 24
TOTAL = float(CELLS * N_CELL)
CARRY = GENES + 16
UNITS = 7


def power_of_two(power):
    size = jnp.abs(power).astype(jnp.int32)
    up = jnp.ones_like(power)
    down = jnp.ones_like(power)
    for bit in range(7):
        on = (size & (1 << bit)) != 0
        up = jnp.where(on, up * 2.0 ** (1 << bit), up)
        down = jnp.where(on, down * 2.0 ** -(1 << bit), down)
    return jnp.where(power < 0, down, up)


def lanes(rows):
    return jnp.concatenate([rows[i : i + 1] for i in range(3)], axis=1)


def kernel(
    x_hbm, out_ref, x_ref, stat, gathered, own, partner, left, right, unscaled, prod, sibling,
    paired, arrived, turned, crossed, row_scale, x_sem, stat_sems, gene_send, gene_recv,
    core_send, core_recv, sum_send, sum_recv, turn_send, turn_recv,
):
    gene = lax.axis_index("gene")
    cell = lax.axis_index("cell")
    core = lax.rem(cell, 2)
    chip = lax.div(cell, 2)
    even = lax.rem(gene, 2) == 0
    here = [jnp.where(even, a, b) for a, b in ((1, 3), (-1, -3), (2, -2))]
    away = [jnp.where(even, a, b) for a, b in ((-3, -1), (3, 1), (-2, 2))]

    def at(offset):
        return lax.rem(gene + offset + N_GENE, N_GENE)

    barrier = pltpu.get_barrier_semaphore()
    for step in range(1, N_CELL):
        pl.semaphore_signal(
            barrier, inc=1, device_id=(gene, lax.rem(cell + step, N_CELL)), device_id_type=MESH
        )
    for offset in (1, -1, 2, -2, 3, -3):
        pl.semaphore_signal(barrier, inc=1, device_id=(at(offset), cell), device_id_type=MESH)

    load = pltpu.make_async_copy(x_hbm, x_ref, x_sem)
    load.start()
    load.wait()
    x = x_ref[...]
    mean = jnp.sum(x, axis=0, keepdims=True) * (1.0 / CELLS)
    centred = x - mean
    rows = [
        mean,
        jnp.sum(centred * centred, axis=0, keepdims=True),
        jnp.max(x, axis=0, keepdims=True),
        jnp.min(x, axis=0, keepdims=True),
    ]
    parts = [row[:, 128 * i : 128 * i + 128] for row in rows for i in range(3)]
    stat[...] = jnp.concatenate(parts + [jnp.zeros((4, 128), jnp.float32)], axis=0)
    gathered[cell] = stat[...]

    pl.semaphore_wait(barrier, 21)

    for step in range(1, N_CELL):
        pltpu.make_async_remote_copy(
            src_ref=stat,
            dst_ref=gathered.at[cell],
            send_sem=stat_sems.at[0],
            recv_sem=stat_sems.at[1],
            device_id=(gene, lax.rem(cell + step, N_CELL)),
            device_id_type=MESH,
        ).start()
    many = gathered.at[pl.ds(0, N_CELL - 1)]
    pltpu.make_async_copy(many, many, stat_sems.at[1]).wait()

    total = gathered[0][0:3]
    for i in range(1, N_CELL):
        total = total + gathered[i][0:3]
    mean3 = total * (1.0 / N_CELL)
    inner = jnp.zeros_like(mean3)
    outer = jnp.zeros_like(mean3)
    high = gathered[0][6:9]
    low = gathered[0][9:12]
    for i in range(N_CELL):
        inner = inner + gathered[i][3:6]
        shift = gathered[i][0:3] - mean3
        outer = outer + shift * shift
        high = jnp.maximum(high, gathered[i][6:9])
        low = jnp.minimum(low, gathered[i][9:12])
    spread = inner + outer * float(CELLS)
    deviation = jnp.sqrt(spread * (1.0 / TOTAL) + EPS)
    peak = jnp.maximum(jnp.abs((high - mean3) / deviation), jnp.abs((low - mean3) / deviation))
    power3 = jnp.ceil(jnp.log2(peak))
    scale3 = power_of_two(-power3)
    power = lanes(power3)
    gain = power_of_two(power)

    standard = (x_ref[...] - lanes(mean3)) / lanes(deviation)
    value = jnp.floor((standard * lanes(scale3)) * 256.0)
    turned_value = value.T
    unscaled[...] = turned_value
    own[0:GENES, :] = turned_value.astype(jnp.bfloat16)
    second = jnp.concatenate([power[:, 256:384], jnp.zeros((1, 128), jnp.float32)], axis=1)
    own[GENES:CARRY, :] = jnp.concatenate(
        [power[:, 0:256], second, jnp.zeros((14, 256), jnp.float32)], axis=0
    ).astype(jnp.bfloat16)

    gene_copies = []
    for slot in range(3):
        copy = pltpu.make_async_remote_copy(
            src_ref=own,
            dst_ref=partner.at[slot],
            send_sem=gene_send.at[slot],
            recv_sem=gene_recv.at[slot],
            device_id=(at(away[slot]), cell),
            device_id_type=MESH,
        )
        copy.start()
        gene_copies.append(copy)

    wide = jnp.broadcast_to(gain * (2.0**-10 / TOTAL), (128, GENES)).T
    row_scale[...] = jnp.concatenate([wide, wide, wide], axis=1)

    def panels(value, slices_ref, sums_ref):
        fourth = value
        third = jnp.floor(fourth * 0.25)
        second = jnp.floor(third * 0.25)
        first = jnp.floor(second * 0.25)
        if slices_ref is not None:
            slices_ref[:, 0:256] = first.astype(jnp.bfloat16)
            slices_ref[:, 256:512] = (second - 4.0 * first).astype(jnp.bfloat16)
            slices_ref[:, 512:768] = (third - 4.0 * second).astype(jnp.bfloat16)
            slices_ref[:, 768:1024] = (fourth - 4.0 * third).astype(jnp.bfloat16)
        sums_ref[:, 0:256] = fourth.astype(jnp.bfloat16)
        sums_ref[:, 256:512] = third.astype(jnp.bfloat16)
        sums_ref[:, 512:768] = second.astype(jnp.bfloat16)
        sums_ref[:, 768:1024] = first.astype(jnp.bfloat16)

    core_copies, sum_copies, turn_copies = {}, {}, {}

    def multiply(unit, a_ref, b_ref):
        c = lax.dot_general(
            a_ref[...], b_ref[...], (((1,), (1,)), ((), ())), preferred_element_type=jnp.float32
        )
        prod[unit] = c.reshape(N_CHIP, 2, ROWS, GENES)
        copy = pltpu.make_async_remote_copy(
            src_ref=prod.at[unit, :, 1 - core],
            dst_ref=sibling.at[unit],
            send_sem=core_send.at[unit],
            recv_sem=core_recv.at[unit],
            device_id=(gene, chip * 2 + 1 - core),
            device_id_type=MESH,
        )
        copy.start()
        core_copies[unit] = copy

    def pair_up(unit):
        core_copies[unit].wait_recv()
        paired[unit] = prod[unit, :, core] + sibling[unit]
        for step in range(1, N_CHIP):
            there = lax.rem(chip + step, N_CHIP)
            copy = pltpu.make_async_remote_copy(
                src_ref=paired.at[unit, there],
                dst_ref=arrived.at[unit, step - 1],
                send_sem=sum_send.at[unit],
                recv_sem=sum_recv.at[unit],
                device_id=(gene, there * 2 + core),
                device_id_type=MESH,
            )
            copy.start()

    def summed(unit):
        pltpu.make_async_copy(arrived.at[unit], arrived.at[unit], sum_recv.at[unit]).wait()
        total = paired[unit, chip]
        for step in range(N_CHIP - 1):
            total = total + arrived[unit, step]
        return total

    mine = pl.ds(pl.multiple_of(cell * ROWS, 8), ROWS)

    def place(offset, block):
        start = pl.multiple_of((offset + 3) * GENES, 128)
        out_ref[:, pl.ds(start, GENES)] = block

    def turn(slot):
        unit = 1 + 2 * slot
        turned[slot] = summed(unit) * gain
        copy = pltpu.make_async_remote_copy(
            src_ref=turned.at[slot],
            dst_ref=crossed.at[slot],
            send_sem=turn_send.at[slot],
            recv_sem=turn_recv.at[slot],
            device_id=(at(here[slot]), cell),
            device_id_type=MESH,
        )
        copy.start()
        turn_copies[slot] = copy

    def keep(slot):
        far = partner[slot, GENES:CARRY, :].astype(jnp.float32)
        far_power = jnp.concatenate([far[0:1, :], far[1:2, 0:128]], axis=1)
        place(here[slot], summed(2 + 2 * slot) * (row_scale[mine, :] * power_of_two(far_power)))

    panels(unscaled[...], left, right.at[3])
    multiply(0, left, right.at[3])
    pair_up(0)
    for slot in range(3):
        gene_copies[slot].wait_recv()
        panels(partner[slot, 0:GENES, :].astype(jnp.float32), None, right.at[slot])
        multiply(1 + 2 * slot, right.at[slot], left)
        multiply(2 + 2 * slot, left, right.at[slot])
        pair_up(1 + 2 * slot)
        pair_up(2 + 2 * slot)
        if slot == 0:
            place(0, summed(0) * (row_scale[mine, :] * gain))
        else:
            turn(slot - 1)
            keep(slot - 1)
    turn(2)
    keep(2)
    for slot in range(3):
        turn_copies[slot].wait_recv()
        place(away[slot], crossed[slot] * row_scale[mine, :])

    pltpu.make_async_copy(many, many, stat_sems.at[0]).wait()
    for slot in range(3):
        gene_copies[slot].wait_send()
        turn_copies[slot].wait_send()
    for unit in range(UNITS):
        core_copies[unit].wait_send()
        pltpu.make_async_copy(arrived.at[unit], arrived.at[unit], sum_send.at[unit]).wait()


def on_device(expression):
    f32, bf16 = jnp.float32, jnp.bfloat16
    vmem, dma = pltpu.VMEM, pltpu.SemaphoreType.DMA
    return pl.pallas_call(
        kernel,
        out_shape=jax.ShapeDtypeStruct((ROWS, UNITS * GENES), f32),
        in_specs=[pl.BlockSpec(memory_space=pl.ANY)],
        out_specs=pl.BlockSpec(memory_space=pltpu.VMEM),
        scratch_shapes=[
            vmem((CELLS, GENES), f32),
            vmem((16, 128), f32),
            vmem((N_CELL, 16, 128), f32),
            vmem((CARRY, CELLS), bf16),
            vmem((3, CARRY, CELLS), bf16),
            vmem((GENES, 4 * CELLS), bf16),
            vmem((4, GENES, 4 * CELLS), bf16),
            vmem((GENES, CELLS), f32),
            vmem((UNITS, N_CHIP, 2, ROWS, GENES), f32),
            vmem((UNITS, N_CHIP, ROWS, GENES), f32),
            vmem((UNITS, N_CHIP, ROWS, GENES), f32),
            vmem((UNITS, N_CHIP - 1, ROWS, GENES), f32),
            vmem((3, ROWS, GENES), f32),
            vmem((3, ROWS, GENES), f32),
            vmem((GENES, GENES), f32),
            dma,
            dma((2,)),
            dma((3,)),
            dma((3,)),
            dma((UNITS,)),
            dma((UNITS,)),
            dma((UNITS,)),
            dma((UNITS,)),
            dma((3,)),
            dma((3,)),
        ],
        compiler_params=pltpu.CompilerParams(
            collective_id=0, has_side_effects=True, vmem_limit_bytes=48 * 1024 * 1024
        ),
        name="banded_correlation",
    )(expression)


def solution(mesh):
    return jax.shard_map(
        on_device,
        mesh=mesh,
        in_specs=(P("cell", "gene"),),
        out_specs=P(("gene", "cell"), None),
        check_vma=False,
    )
```

time: 401 us -> 63.4 us (0.16)
  waiting for transfers between devices: 158 us -> 0 us
  starting transfers between devices: 102 us -> 0 us
  blocking collectives: 87.6 us -> 0 us
  Pallas kernels: 0 us -> 61.1 us
  matrix products: 28.7 us -> 0 us
  between operations: 14.7 us -> 0.01 us
  other arithmetic: 4.56 us -> 0 us
    unnamed x2 -> x0, waiting for transfers between devices: 150 us -> none
    ppermute x14 -> x0, starting transfers between devices: 102 us -> none  [from_behind(): return lax.ppermute(value, axis, pairs)]
    pallas_call x0 -> x1, Pallas kernels: none -> 61.1 us  [on_device(): pl.pallas_call(kernel, out_shape=jax.ShapeDtypeStruct((ROWS, UNITS * GENE...]
    psum x2 -> x0, blocking collectives: 60.5 us -> none  [the longest x1 33.4 us: on_device(): total = lax.psum(jnp.sum(expression, axis=0), 'cell')]
    dot_general x70 -> x0, matrix products: 28.7 us -> none  [contract_cells(): lax.dot_general(left, right, (((0,), (0,)), ((), ())), preferred_element_...]
    pmax x1 -> x0, blocking collectives: 27.1 us -> none  [on_device(): peak = lax.pmax(jnp.max(jnp.abs(standard), axis=0), 'cell')]
    ppermute x14 -> x0, waiting for transfers between devices: 8.44 us -> none  [from_behind(): return lax.ppermute(value, axis, pairs)]
  transfers between devices with their start and end apart: 15 -> 0, of which waited for: 8 -> 0; matrix products, arithmetic and copies ran while one was open for 6% -> 0% of each run, Pallas kernels for 0% -> 0%
where the time goes in v1:
time: 63.4 us; the launch traced here: 62.8 us
  Pallas kernels  61.1 us (96%)
  local copies, waits for them, and re-layouts  1.7 us (3%)
    pallas_call x1, Pallas kernels, on_device(): pl.pallas_call(kernel, out_shape=jax.ShapeDtypeStruct((ROWS, UNITS * GENE...  61.1 us
    unnamed x3, local copies, waits for them, and re-layouts  1.7 us

profile of v1, /device:TPU:1, one launch (start us, length us, event | category | flops | bytes accessed | tf_op | source)
XLA Modules:
  0.0 62.8 jit_solution(1415316274345154575)
XLA Ops:
  0.0 0.0 copy-start
  0.0 1.0 %copy-done = f32[256,384]{1,0:T(8,128)S(1)} copy-done((f32[256,384]{1,0:T(8,128)S(1)}, f32[256,384]{1,0:T(8,128)}, u32[]{:S(2)}) %copy-start) | copy-done | bytes 393240
  1.0 61.1 %banded_correlation.1 = f32[24,2688]{1,0:T(8,128)S(1)} custom-call(f32[256,384]{1,0:T(8,128)S(1)} %copy-done), custom_call_target="tpu_custom_call" | custom-call | tf_op jit(solution)/shard_map/banded_correlation/pallas_call | solution.py:247
  62.1 0.7 %copy.3 = f32[24,2688]{1,0:T(8,128)} copy(f32[24,2688]{1,0:T(8,128)S(1)} %banded_correlation.1) | data formatting | bytes 516096
Async XLA Ops:
  0.0 1.0 %copy-start = (f32[256,384]{1,0:T(8,128)S(1)}, f32[256,384]{1,0:T(8,128)}, u32[]{:S(2)}) copy-start(f32[256,384]{1,0:T(8,128)} %x_hbm.1) | copy-start | bytes 1179652

commit v2 on v1

v2 whole, which is shorter than its diff:
```python
import jax
import jax.numpy as jnp
from jax import lax
from jax.experimental import pallas as pl
from jax.experimental.pallas import tpu as pltpu
from jax.sharding import PartitionSpec as P

EPS = 1e-05
MESH = pl.DeviceIdType.MESH
N_GENE, N_CELL, N_CHIP, N_X = 32, 16, 8, 4
GENES, CELLS, ROWS, PART = 384, 256, 24, 96
TOTAL = float(CELLS * N_CELL)
SLOTS = 3
NEAR = (1, -1, 2, -2, 3, -3)


def power_of_two(power):
    size = jnp.abs(power).astype(jnp.int32)
    up = jnp.ones_like(power)
    down = jnp.ones_like(power)
    for bit in range(7):
        on = (size & (1 << bit)) != 0
        up = jnp.where(on, up * 2.0 ** (1 << bit), up)
        down = jnp.where(on, down * 2.0 ** -(1 << bit), down)
    return jnp.where(power < 0, down, up)


def lanes(rows):
    return jnp.concatenate([rows[i : i + 1] for i in range(3)], axis=1)


def kernel(
    x_hbm, out_ref, x_ref, gathered, block, sent, flat, powers, far_powers, partner, left, right,
    prod, sibling, paired, arrived, turned, turned_sibling, turned_pair, crossed, row_scale,
    x_sem, stat_sems, block_sems, gene_send, gene_recv, power_send, power_recv,
    core_send, core_recv, sum_send, sum_recv, flip_send, flip_recv, turn_send, turn_recv,
):
    gene = lax.axis_index("gene")
    cell = lax.axis_index("cell")
    core = lax.rem(cell, 2)
    chip = lax.div(cell, 2)
    x_at = lax.rem(chip, N_X)
    z_at = lax.div(chip, N_X)
    even = lax.rem(gene, 2) == 0
    here = [jnp.where(even, a, b) for a, b in ((1, 3), (-1, -3), (2, -2))]
    away = [jnp.where(even, a, b) for a, b in ((-3, -1), (3, 1), (-2, 2))]

    def at(offset):
        return lax.rem(gene + offset + N_GENE, N_GENE)

    def rank(z, x, core):
        return z * (2 * N_X) + x * 2 + core

    def remote(src, dst, send, recv, gene_to, cell_to):
        return pltpu.make_async_remote_copy(
            src_ref=src,
            dst_ref=dst,
            send_sem=send,
            recv_sem=recv,
            device_id=(gene_to, cell_to),
            device_id_type=MESH,
        )

    def wait_bytes(ref, sem):
        pltpu.make_async_copy(ref, ref, sem).wait()

    load = pltpu.make_async_copy(x_hbm, x_ref, x_sem)
    load.start()
    barrier = pltpu.get_barrier_semaphore()

    def greet(gene_to, cell_to):
        pl.semaphore_signal(barrier, inc=1, device_id=(gene_to, cell_to), device_id_type=MESH)

    for step in range(1, N_CELL):
        greet(gene, lax.rem(cell + step, N_CELL))
    for offset in NEAR:
        for x in range(N_X):
            greet(at(offset), rank(z_at, x, core))
        greet(at(offset), rank(1 - z_at, x_at, core))

    load.wait()
    x = x_ref[...]
    mean = jnp.sum(x, axis=0, keepdims=True) * (1.0 / CELLS)
    centred = x - mean
    rows = [
        mean,
        jnp.sum(centred * centred, axis=0, keepdims=True),
        jnp.max(x, axis=0, keepdims=True),
        jnp.min(x, axis=0, keepdims=True),
    ]
    parts = [row[:, 128 * i : 128 * i + 128] for row in rows for i in range(3)]
    gathered[cell] = jnp.concatenate(parts + [jnp.zeros((4, 128), jnp.float32)], axis=0)

    pl.semaphore_wait(barrier, N_CELL - 1 + len(NEAR) * (N_X + 1))

    for step in range(1, N_CELL):
        remote(
            gathered.at[cell], gathered.at[cell], stat_sems.at[0], stat_sems.at[1],
            gene, lax.rem(cell + step, N_CELL),
        ).start()
    many = gathered.at[pl.ds(0, N_CELL - 1)]
    wait_bytes(many, stat_sems.at[1])

    total = gathered[0][0:3]
    for i in range(1, N_CELL):
        total = total + gathered[i][0:3]
    mean3 = total * (1.0 / N_CELL)
    inner = jnp.zeros_like(mean3)
    outer = jnp.zeros_like(mean3)
    high = gathered[0][6:9]
    low = gathered[0][9:12]
    for i in range(N_CELL):
        inner = inner + gathered[i][3:6]
        shift = gathered[i][0:3] - mean3
        outer = outer + shift * shift
        high = jnp.maximum(high, gathered[i][6:9])
        low = jnp.minimum(low, gathered[i][9:12])
    spread = inner + outer * float(CELLS)
    deviation = jnp.sqrt(spread * (1.0 / TOTAL) + EPS)
    peak = jnp.maximum(jnp.abs((high - mean3) / deviation), jnp.abs((low - mean3) / deviation))
    power3 = jnp.ceil(jnp.log2(peak))
    scale3 = power_of_two(-power3)
    gain3 = power_of_two(power3)
    gain = lanes(gain3)

    standard = (x_ref[...] - lanes(mean3)) / lanes(deviation)
    value = jnp.floor((standard * lanes(scale3)) * 256.0)
    block[x_at] = value.astype(jnp.bfloat16)
    sent[...] = value.T.astype(jnp.bfloat16).reshape(2, GENES // 2, CELLS)
    powers[...] = jnp.concatenate([gain3, jnp.zeros((5, 128), jnp.float32)], axis=0)

    mine = block.at[x_at]
    for step in (1, 3, 2):
        there = lax.rem(x_at + step, N_X)
        remote(
            mine, mine, block_sems.at[0], block_sems.at[1], gene, rank(z_at, there, core)
        ).start()
    for slot in range(SLOTS):
        for step in range(N_X):
            there = lax.rem(x_at + step, N_X)
            start = pl.multiple_of(there * (PART // 2), 16)
            remote(
                sent.at[:, pl.ds(start, PART // 2)], partner.at[slot, x_at],
                gene_send.at[slot], gene_recv.at[slot], at(away[slot]), rank(z_at, there, core),
            ).start()
        remote(
            powers, far_powers.at[slot], power_send.at[slot], power_recv.at[slot],
            at(away[slot]), cell,
        ).start()

    wide = jnp.broadcast_to(gain * (2.0**-10 / TOTAL), (128, GENES)).T
    row_scale[...] = jnp.concatenate([wide, wide, wide], axis=1)
    mine_rows = pl.ds(pl.multiple_of(cell * ROWS, 8), ROWS)

    def levels(value):
        fourth = value.astype(jnp.float32)
        third = jnp.floor(fourth * 0.25)
        second = jnp.floor(third * 0.25)
        return fourth, third, second, jnp.floor(second * 0.25)

    wait_bytes(block.at[pl.ds(0, N_X - 1)], block_sems.at[1])
    for x in range(N_X):
        fourth, third, second, first = levels(block[x])
        slices = (first, second - 4.0 * first, third - 4.0 * second, fourth - 4.0 * third)
        for i, piece in enumerate(slices):
            start = CELLS * (4 * x + i)
            left[start : start + CELLS, :] = piece.astype(jnp.bfloat16)
        flat[x] = fourth.T.reshape(2, GENES // 2, CELLS)

    core_copies, flip_copies, turn_copies = {}, {}, {}

    def multiply(unit, pieces):
        for x in range(N_X):
            for i, piece in enumerate(levels(pieces(x))):
                start = CELLS * (4 * x + i)
                right[unit, :, start : start + CELLS] = piece.astype(jnp.bfloat16)
        c = jnp.dot(right[unit], left[...], preferred_element_type=jnp.float32)
        if unit < SLOTS:
            turned[unit] = (c * gain).reshape(2, 2, ROWS, GENES)
            copy = remote(
                turned.at[unit, :, 1 - core], turned_sibling.at[unit],
                flip_send.at[unit], flip_recv.at[unit], gene, rank(z_at, x_at, 1 - core),
            )
            copy.start()
            flip_copies[unit] = copy
        prod[unit] = c.T.reshape(N_CHIP, 2, ROWS, PART)
        copy = remote(
            prod.at[unit, :, 1 - core], sibling.at[unit],
            core_send.at[unit], core_recv.at[unit], gene, rank(z_at, x_at, 1 - core),
        )
        copy.start()
        core_copies[unit] = copy

    def pair_up(unit):
        if unit < SLOTS:
            flip_copies[unit].wait_recv()
            turned_pair[unit] = turned[unit, :, core] + turned_sibling[unit]
            turn_copies[unit] = []
            for z in range(2):
                copy = remote(
                    turned_pair.at[unit, z], crossed.at[unit, z_at],
                    turn_send.at[unit], turn_recv.at[unit], at(here[unit]), rank(z, x_at, core),
                )
                copy.start()
        core_copies[unit].wait_recv()
        paired[unit] = prod[unit, :, core] + sibling[unit]
        arrived[unit, chip] = paired[unit, chip]
        for step in range(1, N_CHIP):
            there = lax.rem(chip + step, N_CHIP)
            remote(
                paired.at[unit, there], arrived.at[unit, chip],
                sum_send.at[unit], sum_recv.at[unit], gene, there * 2 + core,
            ).start()

    def place(offset, value):
        start = pl.multiple_of((offset + 3) * GENES, 128)
        out_ref[:, pl.ds(start, GENES)] = value

    def keep(unit, offset, far_gain):
        wait_bytes(arrived.at[unit, pl.ds(0, N_CHIP - 1)], sum_recv.at[unit])
        quarters = [arrived[unit, x] + arrived[unit, N_X + x] for x in range(N_X)]
        half = PART // 2
        total = jnp.concatenate(
            [q[:, half * z : half * (z + 1)] for z in range(2) for q in quarters], axis=1
        )
        place(offset, total * (row_scale[mine_rows, :] * far_gain))

    own_rows = pl.ds(pl.multiple_of(x_at * (PART // 2), 8), PART // 2)
    multiply(SLOTS, lambda x: flat[x, :, own_rows].reshape(PART, CELLS))
    pair_up(SLOTS)
    for slot in range(SLOTS):
        wait_bytes(partner.at[slot], gene_recv.at[slot])
        multiply(slot, lambda x: partner[slot, x].reshape(PART, CELLS))
        if slot:
            pair_up(slot - 1)
    pair_up(SLOTS - 1)
    keep(SLOTS, 0, gain)
    for slot in range(SLOTS):
        wait_bytes(far_powers.at[slot], power_recv.at[slot])
        keep(slot, here[slot], lanes(far_powers[slot][0:3]))
    for slot in range(SLOTS):
        wait_bytes(crossed.at[slot], turn_recv.at[slot])
        place(away[slot], (crossed[slot, 0] + crossed[slot, 1]) * row_scale[mine_rows, :])

    wait_bytes(many, stat_sems.at[0])
    wait_bytes(block.at[pl.ds(0, N_X - 1)], block_sems.at[0])
    for unit in range(SLOTS + 1):
        if unit < SLOTS:
            wait_bytes(sent, gene_send.at[unit])
            wait_bytes(powers, power_send.at[unit])
            flip_copies[unit].wait_send()
            wait_bytes(turned_pair.at[unit], turn_send.at[unit])
        core_copies[unit].wait_send()
        wait_bytes(arrived.at[unit, pl.ds(0, N_CHIP - 1)], sum_send.at[unit])


def on_device(expression):
    f32, bf16 = jnp.float32, jnp.bfloat16
    vmem, dma = pltpu.VMEM, pltpu.SemaphoreType.DMA
    units = SLOTS + 1
    return pl.pallas_call(
        kernel,
        out_shape=jax.ShapeDtypeStruct((ROWS, 7 * GENES), f32),
        in_specs=[pl.BlockSpec(memory_space=pl.ANY)],
        out_specs=pl.BlockSpec(memory_space=pltpu.VMEM),
        scratch_shapes=[
            vmem((CELLS, GENES), f32),
            vmem((N_CELL, 16, 128), f32),
            vmem((N_X, CELLS, GENES), bf16),
            vmem((2, GENES // 2, CELLS), bf16),
            vmem((N_X, 2, GENES // 2, CELLS), f32),
            vmem((8, 128), f32),
            vmem((SLOTS, 8, 128), f32),
            vmem((SLOTS, N_X, 2, PART // 2, CELLS), bf16),
            vmem((4 * CELLS * N_X, GENES), bf16),
            vmem((units, PART, 4 * CELLS * N_X), bf16),
            vmem((units, N_CHIP, 2, ROWS, PART), f32),
            vmem((units, N_CHIP, ROWS, PART), f32),
            vmem((units, N_CHIP, ROWS, PART), f32),
            vmem((units, N_CHIP, ROWS, PART), f32),
            vmem((SLOTS, 2, 2, ROWS, GENES), f32),
            vmem((SLOTS, 2, ROWS, GENES), f32),
            vmem((SLOTS, 2, ROWS, GENES), f32),
            vmem((SLOTS, 2, ROWS, GENES), f32),
            vmem((GENES, GENES), f32),
            dma,
            dma((2,)),
            dma((2,)),
            dma((SLOTS,)),
            dma((SLOTS,)),
            dma((SLOTS,)),
            dma((SLOTS,)),
            dma((units,)),
            dma((units,)),
            dma((units,)),
            dma((units,)),
            dma((SLOTS,)),
            dma((SLOTS,)),
            dma((SLOTS,)),
            dma((SLOTS,)),
        ],
        compiler_params=pltpu.CompilerParams(
            collective_id=0, has_side_effects=True, vmem_limit_bytes=60 * 1024 * 1024
        ),
        name="banded_correlation",
    )(expression)


def solution(mesh):
    return jax.shard_map(
        on_device,
        mesh=mesh,
        in_specs=(P("cell", "gene"),),
        out_specs=P(("gene", "cell"), None),
        check_vma=False,
    )
```

time: 63.4 us -> 55.7 us (0.88)
  Pallas kernels: 61.1 us -> 53.9 us
    pallas_call x1, Pallas kernels: 61.1 us -> 53.9 us  [on_device(): pl.pallas_call(kernel, out_shape=jax.ShapeDtypeStruct((ROWS, 7 * GENES),...]
    unnamed x3 -> x1, local copies, waits for them, and re-layouts: 1.7 us -> 1.66 us
where the time goes in v2:
time: 55.7 us; the launch traced here: 55.5 us
  Pallas kernels  53.9 us (97%)
  local copies, waits for them, and re-layouts  1.66 us (3%)
    pallas_call x1, Pallas kernels, on_device(): pl.pallas_call(kernel, out_shape=jax.ShapeDtypeStruct((ROWS, 7 * GENES),...  53.9 us
    unnamed x1, local copies, waits for them, and re-layouts  1.66 us

profile of v2, /device:TPU:1, one launch (start us, length us, event | category | flops | bytes accessed | tf_op | source)
XLA Modules:
  0.0 55.5 jit_solution(8790125863029000718)
XLA Ops:
  0.0 53.9 %banded_correlation.1 = f32[24,2688]{1,0:T(8,128)} custom-call(f32[256,384]{1,0:T(8,128)} %x_hbm.1), custom_call_target="tpu_custom_call" | custom-call | tf_op jit(solution)/shard_map/banded_correlation/pallas_call | solution.py:261
  53.9 1.7 %copy.3 = f32[24,2688]{1,0:T(8,128)} copy(f32[24,2688]{1,0:T(8,128)} %banded_correlation.1) | data formatting | bytes 516096

commit v3 on v2

v3 whole, which is shorter than its diff:
```python
import jax
import jax.numpy as jnp
from jax import lax
from jax.experimental import pallas as pl
from jax.experimental.pallas import tpu as pltpu
from jax.sharding import PartitionSpec as P

EPS = 1e-05
MESH = pl.DeviceIdType.MESH
N_GENE, N_CELL, N_CHIP, N_X, N_Y = 32, 16, 8, 4, 8
GENES, CELLS, ROWS, PART = 384, 256, 24, 96
TOTAL = float(CELLS * N_CELL)
SLOTS = 3
SLOT_ORDER = (0, 1, 2)
NEAR = (1, -1, 2, -2, 3, -3)


def power_of_two(power):
    size = jnp.abs(power).astype(jnp.int32)
    up = jnp.ones_like(power)
    down = jnp.ones_like(power)
    for bit in range(7):
        on = (size & (1 << bit)) != 0
        up = jnp.where(on, up * 2.0 ** (1 << bit), up)
        down = jnp.where(on, down * 2.0 ** -(1 << bit), down)
    return jnp.where(power < 0, down, up)


def lanes(rows):
    return jnp.concatenate([rows[i : i + 1] for i in range(3)], axis=1)


def kernel(
    x_hbm, out_ref, x_ref, gathered, block, flat, quarter, powers, far_powers, partner, left,
    right, turned, turned_sibling, turned_pair, crossed, prod, sibling, paired, arrived,
    begun, row_scale,
    x_sem, stat_sems, own_send, own_recv, gene_send, gene_recv, power_send, power_recv,
    core_send, core_recv, sum_send, sum_recv, flip_send, flip_recv, turn_send, turn_recv,
):
    gene = lax.axis_index("gene")
    cell = lax.axis_index("cell")
    core = lax.rem(cell, 2)
    chip = lax.div(cell, 2)
    x_at = lax.rem(chip, N_X)
    z_at = lax.div(chip, N_X)
    even = lax.rem(gene, 2) == 0
    place_y = lax.rem(gene, N_Y)

    def by_place(for_even, for_odd, **special):
        value = jnp.where(even, for_even, for_odd)
        for name, other in special.items():
            value = jnp.where(place_y == int(name[1:]), other, value)
        return value

    here = [by_place(1, 3, y7=2), by_place(-1, -3, y2=-3), by_place(2, -2, y1=1)]
    back = [by_place(0, 0, y7=1), by_place(1, 1, y2=2), by_place(2, 2, y1=0)]
    away = [by_place(-3, -1, y2=-1), by_place(3, 1, y1=-2), by_place(-2, 2, y7=3)]
    slot_there = [by_place(0, 0, y2=2), by_place(1, 1, y1=0), by_place(2, 2, y7=1)]

    def at(offset):
        return lax.rem(gene + offset + N_GENE, N_GENE)

    def rank(z, x, core):
        return z * (2 * N_X) + x * 2 + core

    def remote(src, dst, send, recv, gene_to, cell_to):
        return pltpu.make_async_remote_copy(
            src_ref=src,
            dst_ref=dst,
            send_sem=send,
            recv_sem=recv,
            device_id=(gene_to, cell_to),
            device_id_type=MESH,
        )

    def wait_bytes(ref, sem):
        pltpu.make_async_copy(ref, ref, sem).wait()

    load = pltpu.make_async_copy(x_hbm, x_ref, x_sem)
    load.start()
    barrier = pltpu.get_barrier_semaphore()

    def greet(gene_to, cell_to):
        pl.semaphore_signal(barrier, inc=1, device_id=(gene_to, cell_to), device_id_type=MESH)

    for step in range(1, N_CELL):
        greet(gene, lax.rem(cell + step, N_CELL))
    for offset in NEAR:
        for z in range(2):
            greet(at(offset), rank(z, x_at, core))

    load.wait()
    x = x_ref[...]
    mean = jnp.sum(x, axis=0, keepdims=True) * (1.0 / CELLS)
    centred = x - mean
    rows = [
        mean,
        jnp.sum(centred * centred, axis=0, keepdims=True),
        jnp.max(x, axis=0, keepdims=True),
        jnp.min(x, axis=0, keepdims=True),
    ]
    parts = [row[:, 128 * i : 128 * i + 128] for row in rows for i in range(3)]
    gathered[cell] = jnp.concatenate(parts + [jnp.zeros((4, 128), jnp.float32)], axis=0)

    pl.semaphore_wait(barrier, N_CELL - 1 + len(NEAR) * 2)

    for step in range(1, N_CELL):
        remote(
            gathered.at[cell], gathered.at[cell], stat_sems.at[0], stat_sems.at[1],
            gene, lax.rem(cell + step, N_CELL),
        ).start()
    many = gathered.at[pl.ds(0, N_CELL - 1)]
    wait_bytes(many, stat_sems.at[1])

    total = gathered[0][0:3]
    for i in range(1, N_CELL):
        total = total + gathered[i][0:3]
    mean3 = total * (1.0 / N_CELL)
    inner = jnp.zeros_like(mean3)
    outer = jnp.zeros_like(mean3)
    high = gathered[0][6:9]
    low = gathered[0][9:12]
    for i in range(N_CELL):
        inner = inner + gathered[i][3:6]
        shift = gathered[i][0:3] - mean3
        outer = outer + shift * shift
        high = jnp.maximum(high, gathered[i][6:9])
        low = jnp.minimum(low, gathered[i][9:12])
    spread = inner + outer * float(CELLS)
    deviation = jnp.sqrt(spread * (1.0 / TOTAL) + EPS)
    peak = jnp.maximum(jnp.abs((high - mean3) / deviation), jnp.abs((low - mean3) / deviation))
    power3 = jnp.ceil(jnp.log2(peak))
    scale3 = power_of_two(-power3)
    gain3 = power_of_two(power3)
    gain = lanes(gain3)

    standard = (x_ref[...] - lanes(mean3)) / lanes(deviation)
    value = jnp.floor((standard * lanes(scale3)) * 256.0)
    block[x_at] = value.astype(jnp.bfloat16)
    powers[...] = jnp.concatenate([gain3, jnp.zeros((5, 128), jnp.float32)], axis=0)

    x_of = [lax.rem(x_at + step, N_X) for step in range(N_X)]
    mine = block.at[x_at]
    for step, side in ((1, 0), (3, 1)):
        remote(
            mine, mine, own_send.at[0], own_recv.at[side], gene, rank(z_at, x_of[step], core)
        ).start()
    part_rows = pl.ds(pl.multiple_of(x_at * (PART // 2), 8), PART // 2)

    def send_quarter(step, values):
        flat[...] = values.T.reshape(2, GENES // 2, CELLS)
        quarter[step] = flat[:, part_rows].astype(jnp.bfloat16)
        for slot in range(SLOTS):
            remote(
                quarter.at[step], partner.at[slot_there[slot], step], gene_send.at[slot],
                gene_recv.at[slot_there[slot], step], at(away[slot]), cell,
            ).start()

    send_quarter(0, value)
    for slot in range(SLOTS):
        remote(
            powers, far_powers.at[slot_there[slot]], power_send.at[slot],
            power_recv.at[slot_there[slot]], at(away[slot]), cell,
        ).start()

    wide = jnp.broadcast_to(gain * (2.0**-10 / TOTAL), (128, GENES)).T
    row_scale[...] = jnp.concatenate([wide, wide, wide], axis=1)
    mine_rows = pl.ds(pl.multiple_of(cell * ROWS, 8), ROWS)

    def levels(value):
        fourth = value.astype(jnp.float32)
        third = jnp.floor(fourth * 0.25)
        second = jnp.floor(third * 0.25)
        return fourth, third, second, jnp.floor(second * 0.25)

    chunk = 4 * CELLS
    order = (0, 3, 1, 2)

    def spread_out(step, values):
        fourth, third, second, first = levels(values)
        slices = (first, second - 4.0 * first, third - 4.0 * second, fourth - 4.0 * third)
        for i, piece in enumerate(slices):
            start = chunk * order.index(step) + CELLS * i
            left[start : start + CELLS, :] = piece.astype(jnp.bfloat16)

    def sums_of(ref, row, piece, step):
        for i, level in enumerate(levels(piece.reshape(PART, CELLS))):
            start = chunk * order.index(step) + CELLS * i
            ref[row : row + PART, start : start + CELLS] = level.astype(jnp.bfloat16)

    spread_out(0, value)
    half = CELLS // 2
    for side, came, to in ((0, 3, 1), (1, 1, 3)):
        wait_bytes(block.at[0], own_recv.at[side])
        piece = block.at[x_of[came], pl.ds(side * half, half)]
        remote(
            piece, piece, own_send.at[1], own_recv.at[2 + side], gene, rank(z_at, x_of[to], core)
        ).start()
        send_quarter(came, block[x_of[came]].astype(jnp.float32))
    for step in (3, 1):
        spread_out(step, block[x_of[step]])
    for side in range(2):
        wait_bytes(block.at[0, pl.ds(0, half)], own_recv.at[2 + side])
    send_quarter(2, block[x_of[2]].astype(jnp.float32))
    spread_out(2, block[x_of[2]])

    twin = rank(z_at, x_at, 1 - core)

    copies = {}

    early = chunk * (N_X - 1)

    def product(rows, columns):
        return jnp.dot(right[rows, columns], left[columns], preferred_element_type=jnp.float32)

    def multiply(unit):
        rows = slice(PART * unit, PART * (unit + 1))
        if unit == SLOTS:
            c = product(rows, slice(None))
        else:
            c = begun[rows] + product(rows, slice(early, None))
        if unit < SLOTS:
            turned[unit] = (c * gain).reshape(2, 2, ROWS, GENES)
            copies["flip", unit] = remote(
                turned.at[unit, :, 1 - core], turned_sibling.at[unit],
                flip_send.at[unit], flip_recv.at[unit], gene, twin,
            )
            copies["flip", unit].start()
        prod[unit] = c.T.reshape(N_CHIP, 2, ROWS, PART)
        copies["core", unit] = remote(
            prod.at[unit, :, 1 - core], sibling.at[unit],
            core_send.at[unit], core_recv.at[unit], gene, twin,
        )
        copies["core", unit].start()

    def pair_up(unit):
        if unit < SLOTS:
            copies["flip", unit].wait_recv()
            turned_pair[unit] = turned[unit, :, core] + turned_sibling[unit]
            for z in range(2):
                remote(
                    turned_pair.at[unit, z], crossed.at[back[unit], z_at], turn_send.at[unit],
                    turn_recv.at[back[unit]], at(here[unit]), rank(z, x_at, core),
                ).start()
        copies["core", unit].wait_recv()
        paired[unit] = prod[unit, :, core] + sibling[unit]
        arrived[unit, chip] = paired[unit, chip]
        for step in range(1, N_CHIP):
            there = lax.rem(chip + step, N_CHIP)
            remote(
                paired.at[unit, there], arrived.at[unit, chip],
                sum_send.at[unit], sum_recv.at[unit], gene, there * 2 + core,
            ).start()

    for step in order:
        sums_of(right, PART * SLOTS, quarter[step], step)
    multiply(SLOTS)

    def take(slot, step):
        wait_bytes(partner.at[slot, step], gene_recv.at[slot, step])
        sums_of(right, PART * slot, partner[slot, step], step)

    for step in order[:-1]:
        for slot in SLOT_ORDER:
            take(slot, step)
    begun[...] = product(slice(0, PART * SLOTS), slice(0, early))
    for i, slot in enumerate(SLOT_ORDER):
        take(slot, order[-1])
        multiply(slot)
        pair_up(SLOT_ORDER[i - 1] if i else SLOTS)
    pair_up(SLOT_ORDER[-1])

    def place(offset, value):
        start = pl.multiple_of((offset + 3) * GENES, 128)
        out_ref[:, pl.ds(start, GENES)] = value

    others = pl.ds(0, N_CHIP - 1)

    def keep(unit, offset, far_gain):
        wait_bytes(arrived.at[unit, others], sum_recv.at[unit])
        quarters = [arrived[unit, x] + arrived[unit, N_X + x] for x in range(N_X)]
        size = PART // 2
        total = jnp.concatenate(
            [q[:, size * z : size * (z + 1)] for z in range(2) for q in quarters], axis=1
        )
        place(offset, total * (row_scale[mine_rows, :] * far_gain))

    keep(SLOTS, 0, gain)
    for slot in SLOT_ORDER:
        wait_bytes(far_powers.at[slot], power_recv.at[slot])
        keep(slot, here[slot], lanes(far_powers[slot][0:3]))
    for slot in range(SLOTS):
        wait_bytes(crossed.at[slot], turn_recv.at[slot])
        place(away[slot], (crossed[slot, 0] + crossed[slot, 1]) * row_scale[mine_rows, :])

    wait_bytes(many, stat_sems.at[0])
    wait_bytes(block.at[pl.ds(0, 2)], own_send.at[0])
    wait_bytes(block.at[0], own_send.at[1])
    for unit in range(SLOTS + 1):
        if unit < SLOTS:
            wait_bytes(quarter, gene_send.at[unit])
            wait_bytes(powers, power_send.at[unit])
            wait_bytes(turned_pair.at[unit], turn_send.at[unit])
            copies["flip", unit].wait_send()
        copies["core", unit].wait_send()
        wait_bytes(arrived.at[unit, others], sum_send.at[unit])


def on_device(expression):
    f32, bf16 = jnp.float32, jnp.bfloat16
    vmem, dma = pltpu.VMEM, pltpu.SemaphoreType.DMA
    return pl.pallas_call(
        kernel,
        out_shape=jax.ShapeDtypeStruct((ROWS, 7 * GENES), f32),
        in_specs=[pl.BlockSpec(memory_space=pl.ANY)],
        out_specs=pl.BlockSpec(memory_space=pltpu.VMEM),
        scratch_shapes=[
            vmem((CELLS, GENES), f32),
            vmem((N_CELL, 16, 128), f32),
            vmem((N_X, CELLS, GENES), bf16),
            vmem((2, GENES // 2, CELLS), f32),
            vmem((N_X, 2, PART // 2, CELLS), bf16),
            vmem((8, 128), f32),
            vmem((SLOTS, 8, 128), f32),
            vmem((SLOTS, N_X, 2, PART // 2, CELLS), bf16),
            vmem((4 * CELLS * N_X, GENES), bf16),
            vmem(((SLOTS + 1) * PART, 4 * CELLS * N_X), bf16),
            vmem((SLOTS, 2, 2, ROWS, GENES), f32),
            vmem((SLOTS, 2, ROWS, GENES), f32),
            vmem((SLOTS, 2, ROWS, GENES), f32),
            vmem((SLOTS, 2, ROWS, GENES), f32),
            vmem((SLOTS + 1, N_CHIP, 2, ROWS, PART), f32),
            vmem((SLOTS + 1, N_CHIP, ROWS, PART), f32),
            vmem((SLOTS + 1, N_CHIP, ROWS, PART), f32),
            vmem((SLOTS + 1, N_CHIP, ROWS, PART), f32),
            vmem((SLOTS * PART, GENES), f32),
            vmem((GENES, GENES), f32),
            dma,
            dma((2,)),
            dma((2,)),
            dma((4,)),
            dma((SLOTS,)),
            dma((SLOTS, N_X)),
            dma((SLOTS,)),
            dma((SLOTS,)),
            dma((SLOTS + 1,)),
            dma((SLOTS + 1,)),
            dma((SLOTS + 1,)),
            dma((SLOTS + 1,)),
            dma((SLOTS,)),
            dma((SLOTS,)),
            dma((SLOTS,)),
            dma((SLOTS,)),
        ],
        compiler_params=pltpu.CompilerParams(
            collective_id=0, has_side_effects=True, vmem_limit_bytes=54784 * 1024
        ),
        name="banded_correlation",
    )(expression)


def solution(mesh):
    return jax.shard_map(
        on_device,
        mesh=mesh,
        in_specs=(P("cell", "gene"),),
        out_specs=P(("gene", "cell"), None),
        check_vma=False,
    )
```

time: 55.7 us -> 53.3 us (0.957)
  Pallas kernels: 53.9 us -> 52.2 us
  local copies, waits for them, and re-layouts: 1.66 us -> 0.7 us
    pallas_call x1, Pallas kernels: 53.9 us -> 52.2 us  [on_device(): pl.pallas_call(kernel, out_shape=jax.ShapeDtypeStruct((ROWS, 7 * GENES),...]
    unnamed x1, local copies, waits for them, and re-layouts: 1.66 us -> 0.7 us
where the time goes in v3:
time: 53.3 us; the launch traced here: 52.9 us
  Pallas kernels  52.2 us (98%)
  local copies, waits for them, and re-layouts  0.7 us (1%)
    pallas_call x1, Pallas kernels, on_device(): pl.pallas_call(kernel, out_shape=jax.ShapeDtypeStruct((ROWS, 7 * GENES),...  52.2 us

profile of v3, /device:TPU:1, one launch (start us, length us, event | category | flops | bytes accessed | tf_op | source)
XLA Modules:
  0.0 52.9 jit_solution(4024454828051316238)
XLA Ops:
  0.0 52.2 %banded_correlation.1 = f32[24,2688]{1,0:T(8,128)S(1)} custom-call(f32[256,384]{1,0:T(8,128)} %x_hbm.1), custom_call_target="tpu_custom_call" | custom-call | tf_op jit(solution)/shard_map/banded_correlation/pallas_call | solution.py:312
  52.2 0.7 %copy.3 = f32[24,2688]{1,0:T(8,128)} copy(f32[24,2688]{1,0:T(8,128)S(1)} %banded_correlation.1) | data formatting | bytes 516096

commit v4 on v3

--- a/solution.py
+++ b/solution.py
@@ -11,8 +11,9 @@
 GENES, CELLS, ROWS, PART = 384, 256, 24, 96
 TOTAL = float(CELLS * N_CELL)
 SLOTS = 3
-SLOT_ORDER = (0, 1, 2)
-NEAR = (1, -1, 2, -2, 3, -3)
+SLOT_ORDER = (0, 2, 1)
+NEAR = (3, -3, 2, -2, 1, -1)
+FAR_FIRST = (12, 13, 11, 4, 5, 3, 10, 9, 14, 6, 7, 2, 8, 15, 1)
 
 
 def power_of_two(power):
@@ -83,11 +84,11 @@
     def greet(gene_to, cell_to):
         pl.semaphore_signal(barrier, inc=1, device_id=(gene_to, cell_to), device_id_type=MESH)
 
-    for step in range(1, N_CELL):
-        greet(gene, lax.rem(cell + step, N_CELL))
     for offset in NEAR:
         for z in range(2):
             greet(at(offset), rank(z, x_at, core))
+    for step in range(1, N_CELL):
+        greet(gene, lax.rem(cell + step, N_CELL))
 
     load.wait()
     x = x_ref[...]
@@ -104,7 +105,7 @@
 
     pl.semaphore_wait(barrier, N_CELL - 1 + len(NEAR) * 2)
 
-    for step in range(1, N_CELL):
+    for step in FAR_FIRST:
         remote(
             gathered.at[cell], gathered.at[cell], stat_sems.at[0], stat_sems.at[1],
             gene, lax.rem(cell + step, N_CELL),

time: 53.3 us -> 53.1 us (level)
  no operation moved by 1% of the time
where the time goes in v4:
time: 53.1 us; the launch traced here: 52.9 us
  Pallas kernels  52.2 us (98%)
  local copies, waits for them, and re-layouts  0.7 us (1%)
    pallas_call x1, Pallas kernels, on_device(): pl.pallas_call(kernel, out_shape=jax.ShapeDtypeStruct((ROWS, 7 * GENES),...  52.2 us

profile of v4, /device:TPU:1, one launch (start us, length us, event | category | flops | bytes accessed | tf_op | source)
XLA Modules:
  0.0 52.9 jit_solution(10408528587922486612)
XLA Ops:
  0.0 52.2 %banded_correlation.1 = f32[24,2688]{1,0:T(8,128)S(1)} custom-call(f32[256,384]{1,0:T(8,128)} %x_hbm.1), custom_call_target="tpu_custom_call" | custom-call | tf_op jit(solution)/shard_map/banded_correlation/pallas_call | solution.py:313
  52.2 0.7 %copy.3 = f32[24,2688]{1,0:T(8,128)} copy(f32[24,2688]{1,0:T(8,128)S(1)} %banded_correlation.1) | data formatting | bytes 516096
